TPU v7x, 32 devices: a whole 2x2x4 slice. The times are simulated.
32 devices in a mesh: groups: 2 (over y), dom: 4 (over z), feat: 2 (over x), sub: 2 (over core).
Axes of the slice: x: 2, y: 2, z: 4, core: 2. Of those that a mesh axis runs over, the one named last changes fastest.
Arguments:
- grid_latent: bfloat16 [16384, 512], P(('groups', 'dom')), parts along dimension 0, may hold values from -6 to 6
- mesh_latent: bfloat16 [6144, 512], P(('groups', 'dom'), 'feat'), parts along dimension 0, may hold values from -6 to 6
- encoder_tiles: int32 [2, 256], P(None, ('dom', 'sub')), may hold values from 0 to 31, as said below
- encoder_lanes: int32 [16384], P(('dom', 'sub')), may hold values from 0 to 63, as said below
- encoder_geometry: float32 [4, 16384], P(None, ('dom', 'sub')), may hold values from -6 to 6
- halo_tiles: int32 [4, 4, 3], P('dom'), may hold values from -1 to 11, as said below
- mesh_tiles: int32 [2, 192], P(None, ('dom', 'sub')), may hold values from 0 to 23, as said below
- mesh_lanes: int32 [12288], P(('dom', 'sub')), may hold values from 0 to 63, as said below
- mesh_geometry: float32 [4, 12288], P(None, ('dom', 'sub')), may hold values from -6 to 6
- sender_weight: bfloat16 [3, 512, 512], P(None, None, 'feat'), may hold values from -0.25 to 0.25
- receiver_weight: bfloat16 [3, 512, 512], P(None, None, 'feat'), may hold values from -0.25 to 0.25
- node_weight: bfloat16 [3, 512, 512], P(None, None, 'feat'), may hold values from -0.25 to 0.25
- edge_weight: float32 [3, 4, 512], P(None, None, 'feat'), may hold values from -3 to 3
- edge_bias: float32 [3, 512], P(None, 'feat'), may hold values from -3 to 3
- node_bias: float32 [3, 512], P(None, 'feat'), may hold values from -3 to 3
- output_weight: bfloat16 [3, 512, 512], P(None, None, 'feat'), may hold values from -4 to 4
- norm_gain: float32 [3, 512], P(None, 'feat'), may hold values from 0.1 to 1.9
Outputs:
- mesh_out: bfloat16 [6144, 512], P(('groups', 'dom'), 'feat'), parts along dimension 0
There are 2 independent parts, one for each index of `groups`. A program takes and returns all parts, laid end to end along the dimension named above; an argument that names none is the same for every part. Nothing has to cross between parts.
Inputs may be any that keep to these rules, and one draw needn't show every extreme that they name: `encoder_tiles`: row 0 names source grid tiles below 32, each tile of a partition named by exactly 2 of its blocks; row 1 names destination mesh tiles below 12, each named at least once in a partition. Partition p's blocks are those that dom index p holds. `encoder_lanes`: the lanes of one block are a permutation of 0 .. 63. `halo_tiles`: entry [p, q, c] is the c-th mesh tile that partition p sends to partition q, a tile below 12, or -1 for an empty slot. Only q = p + 1, q = p - 1 and q = p + 4 // 2 modulo 4 hold tiles; a list's tiles are distinct and fill its first slots; each such list holds at least one tile, and some list holds 3 in every draw. `mesh_tiles`: row 0: a source below M = 12 is a local tile; a larger one s names slot (s - M) % 3 of the list that partition (s - M) // 3 sends to this partition, always a filled slot, and every filled slot is named by exactly one block of the receiving partition; every local tile is named at least once. Row 1: destination tiles, each named by exactly 4 blocks of the partition. `mesh_lanes`: the lanes of one block are a permutation of 0 .. 63.
All inputs are finite; a program needn't handle non-finite values.
Results may differ from a plain program's by a relative error of at most 0.0064.
Values may be sent and summed in bfloat16 or wider, within the bound.
A program may use at most 64 MiB of HBM per device.

v0:
```python
import jax
import jax.numpy as jnp
from jax import lax
from jax.sharding import PartitionSpec as P

TILE = 64
LAYERS = 3


EPSILON = 1e-05


def widen_latent(latent, weights):
    portion = lax.all_gather(latent, "feat", axis=1, tiled=True)
    return tuple(
        (jnp.dot(portion, weight, preferred_element_type=jnp.float32) for weight in weights)
    )


def edge_sum(geometry, edge_rows, bias_row, source_values, receivers, target_tiles, tile_count):
    blocks = target_tiles.shape[0]
    geometry_term = jnp.einsum("ce,ch->eh", geometry, edge_rows, precision=lax.Precision.HIGHEST)
    columns = geometry_term.shape[1]
    receiver_tiles = receivers.reshape(tile_count, TILE, columns)
    before = (geometry_term + source_values.astype(jnp.float32) + bias_row).reshape(
        blocks, TILE, columns
    )
    before = before + jnp.take(receiver_tiles, target_tiles, axis=0)
    message = jax.nn.silu(before)
    selector = (target_tiles[:, None] == jnp.arange(tile_count, dtype=jnp.int32)[None, :]).astype(
        jnp.float32
    )
    summed = jnp.einsum("bt,bjh->tjh", selector, message, precision=lax.Precision.HIGHEST)
    return summed.reshape(tile_count * TILE, columns)


def local(
    grid_latent,
    mesh_latent,
    encoder_tiles,
    encoder_lanes,
    encoder_geometry,
    halo_tiles,
    mesh_tiles,
    mesh_lanes,
    mesh_geometry,
    sender_weight,
    receiver_weight,
    node_weight,
    edge_weight,
    edge_bias,
    node_bias,
    output_weight,
    norm_gain,
):
    partitions = lax.axis_size("dom")
    model_width = sender_weight.shape[1]
    hidden_share = sender_weight.shape[2]
    grid_count = grid_latent.shape[0]
    band_share = grid_count // partitions
    mesh_count = mesh_latent.shape[0]
    tile_count = mesh_count // TILE
    arrived = lax.all_to_all(
        grid_latent.reshape(partitions, band_share, model_width),
        "dom",
        split_axis=0,
        concat_axis=0,
        tiled=True,
    )
    senders = jnp.dot(
        arrived.reshape(grid_count, model_width),
        sender_weight[0],
        preferred_element_type=jnp.float32,
    )
    latent = mesh_latent
    for layer_index in range(LAYERS):
        if layer_index == 0:
            receivers, base_term = widen_latent(latent, (receiver_weight[0], node_weight[0]))
            sender_table = senders
            tile_pairs = encoder_tiles
            lane_list = encoder_lanes
            geometry = encoder_geometry
            source_tile = encoder_tiles[0]
        else:
            local_send, receivers, base_term = widen_latent(
                latent,
                (
                    sender_weight[layer_index],
                    receiver_weight[layer_index],
                    node_weight[layer_index],
                ),
            )
            sent_tiles = local_send.astype(jnp.bfloat16).reshape(tile_count, TILE, hidden_share)
            source_tile = mesh_tiles[0]
            listing = halo_tiles[0]
            outgoing = jnp.take(sent_tiles, jnp.maximum(listing, 0), axis=0)
            incoming = lax.all_to_all(outgoing, "dom", split_axis=0, concat_axis=0, tiled=True)
            table_tiles = jnp.concatenate(
                [sent_tiles, incoming.reshape(-1, TILE, hidden_share)], axis=0
            )
            sender_table = table_tiles.reshape(-1, hidden_share)
            tile_pairs = mesh_tiles
            lane_list = mesh_lanes
            geometry = mesh_geometry
        blocks = tile_pairs.shape[1]
        source_rows = (TILE * source_tile[:, None] + lane_list.reshape(blocks, TILE)).reshape(-1)
        gathered_rows = jnp.take(sender_table, source_rows, axis=0)
        partial_value = edge_sum(
            geometry,
            edge_weight[layer_index],
            edge_bias[layer_index],
            gathered_rows,
            receivers,
            tile_pairs[1],
            tile_count,
        )
        incoming_sum = lax.psum_scatter(partial_value, "sub", scatter_dimension=0, tiled=True)
        half_rows = incoming_sum.shape[0]
        first_row = lax.axis_index("sub") * half_rows
        base_rows = lax.dynamic_slice_in_dim(base_term, first_row, half_rows, 0)
        latent_rows = lax.dynamic_slice_in_dim(latent, first_row, half_rows, 0)
        hidden = jax.nn.silu(base_rows + incoming_sum + node_bias[layer_index]).astype(jnp.bfloat16)
        out_weight = output_weight[layer_index]
        update = jnp.dot(
            lax.all_gather(hidden, "feat", axis=1, tiled=True),
            out_weight,
            preferred_element_type=jnp.float32,
        )
        row_sum, row_squares = lax.psum(
            (jnp.sum(update, axis=1), jnp.sum(update * update, axis=1)), "feat"
        )
        row_mean = row_sum / model_width
        variance = row_squares / model_width - row_mean * row_mean
        normed = (
            (update - row_mean[:, None])
            * lax.rsqrt(variance + EPSILON)[:, None]
            * norm_gain[layer_index]
        )
        renewed = (latent_rows.astype(jnp.float32) + normed).astype(jnp.bfloat16)
        latent = lax.all_gather(renewed, "sub", axis=0, tiled=True)
    return latent


def solution(mesh):
    in_specs = (
        P(("groups", "dom"), None),
        P(("groups", "dom"), "feat"),
        P(None, ("dom", "sub")),
        P(("dom", "sub")),
        P(None, ("dom", "sub")),
        P("dom", None, None),
        P(None, ("dom", "sub")),
        P(("dom", "sub")),
        P(None, ("dom", "sub")),
        P(None, None, "feat"),
        P(None, None, "feat"),
        P(None, None, "feat"),
        P(None, None, "feat"),
        P(None, "feat"),
        P(None, "feat"),
        P(None, None, "feat"),
        P(None, "feat"),
    )
    out_specs = P(("groups", "dom"), "feat")
    return jax.shard_map(local, mesh=mesh, in_specs=in_specs, out_specs=out_specs, check_vma=False)
```

profile of v0, /device:TPU:0, one launch (start us, length us, event | category | flops | bytes accessed | tf_op | source)
XLA Modules:
  0.0 252.4 jit_solution(6584619567084079083)
XLA Ops:
  6.5 6.5 %all-to-all-start = ((bf16[4,512,512]{2,1,0:T(8,128)(2,1)}), bf16[4,512,512]{2,1,0:T(8,128)(2,1)S(1)}, u32[]{:S(2)}, u32[]{:S(2)}) async-start(bf16[4,512,512]{2,1,0:T(8,128)(2,1)} %bitcast.137), calls=%async_computation | async-start | bytes 4194304 | tf_op jit(solution)/shard_map/all_to_all | solution.py:63
  13.6 11.3 %all_gather.27 = bf16[768,512]{1,0:T(8,128)(2,1)S(1)} all-gather(bf16[768,256]{1,0:T(8,128)(2,1)S(1)} %copy-done.11), channel_id=1, replica_groups=mesh['groups'=2,'dom'=4,'feat'=2,'sub'=2] {'feat'}, dimensions={1}, use_global_device_ids=true | all-gather | bytes 1179648 | tf_op jit(solution)/shard_map/all_gather | solution.py:14
  29.1 32.1 %all-to-all-done = bf16[4,512,512]{2,1,0:T(8,128)(2,1)S(1)} async-done(((bf16[4,512,512]{2,1,0:T(8,128)(2,1)}), bf16[4,512,512]{2,1,0:T(8,128)(2,1)S(1)}, u32[]{:S(2)}, u32[]{:S(2)}) %all-to-all-start) | async-done | bytes 2097184 | tf_op jit(solution)/shard_map/all_to_all | solution.py:63
  64.8 8.6 %gather_fusion = f32[2048,256]{1,0:T(8,128)} fusion(f32[2048,256]{1,0:T(8,128)S(1)} %fusion.27, s32[2048]{0:T(1024)S(1)} %broadcast_clamp_fusion), kind=kCustom, calls=%fused_computation.6 | custom fusion | bytes 4202496 | tf_op jit(solution)/shard_map/jit(_take)/gather | solution.py:107
  73.4 3.7 %fusion.2 = f32[2048,256]{1,0:T(8,128)S(1)} fusion(f32[4,2048]{1,0:T(4,128)S(1)} %copy-done, f32[2048,256]{1,0:T(8,128)} %gather_fusion, f32[256]{0:T(256)S(1)} %bitcast.149, pred[2048]{0:T(1024)(128)(4,1)S(1)} %compare_and_fusion.1, f32[3,4,256]{2,1,0:T(4,128)S(1)} %copy-done.14), kind=kOutput, calls=%fused_computation.13 | convolution fusion | flops 26738688 | bytes 4234240 | tf_op jit(solution)/shard_map/ce,ch->eh/dot_general | solution.py:22
  82.9 5.9 %reduce-scatter.4.cloned.1.call-done = f32[384,256]{1,0:T(8,128)} async-done(((f32[768,256]{1,0:T(8,128)}), f32[384,256]{1,0:T(8,128)}) %reduce-scatter.4.cloned.1.call-update) | async-done | bytes 393232 | tf_op jit(solution)/shard_map/reduce_scatter | solution.py:117
  90.0 7.7 %all_gather.28 = bf16[384,512]{1,0:T(8,128)(2,1)S(1)} all-gather(bf16[384,256]{1,0:T(8,128)(2,1)S(1)} %multiply_convert_fusion.2), channel_id=1, replica_groups=mesh['groups'=2,'dom'=4,'feat'=2,'sub'=2] {'feat'}, dimensions={1}, use_global_device_ids=true | all-gather | bytes 589824 | tf_op jit(solution)/shard_map/all_gather | solution.py:125
  99.0 4.9 %all-reduce.2 = (f32[384]{0:T(512)S(1)}, f32[384]{0:T(512)S(1)}) all-reduce(f32[384]{0:T(512)S(1)} %get-tuple-element.13, f32[384]{0:T(512)S(1)} %get-tuple-element.12), channel_id=1, replica_groups=mesh['groups'=2,'dom'=4,'feat'=2,'sub'=2] {'feat'}, use_global_device_ids=true, to_apply=%region_4.5 | all-reduce | flops 768 | bytes 6144 | tf_op jit(solution)/shard_map/psum | solution.py:129
  106.9 11.8 %all_gather.30 = bf16[768,512]{0,1:T(8,128)(2,1)S(1)} all-gather(bf16[768,256]{0,1:T(8,128)(2,1)S(1)} %all_gather.29), channel_id=1, replica_groups=mesh['groups'=2,'dom'=4,'feat'=2,'sub'=2] {'feat'}, dimensions={1}, use_global_device_ids=true | all-gather | bytes 1179648 | tf_op jit(solution)/shard_map/all_gather | solution.py:14
  121.6 4.9 %all-to-all-start.1 = ((bf16[4,3,64,256]{3,2,1,0:T(8,128)(2,1)}), bf16[4,3,64,256]{3,2,1,0:T(8,128)(2,1)}, u32[]{:S(2)}, u32[]{:S(2)}) async-start(bf16[4,3,64,256]{3,2,1,0:T(8,128)(2,1)} %broadcast_select_fusion.1), calls=%async_computation.2 | async-start | bytes 786432 | tf_op jit(solution)/shard_map/all_to_all | solution.py:97
  128.8 8.9 %all-to-all-done.1 = bf16[4,3,64,256]{3,2,1,0:T(8,128)(2,1)} async-done(((bf16[4,3,64,256]{3,2,1,0:T(8,128)(2,1)}), bf16[4,3,64,256]{3,2,1,0:T(8,128)(2,1)}, u32[]{:S(2)}, u32[]{:S(2)}) %all-to-all-start.1) | async-done | bytes 393248 | tf_op jit(solution)/shard_map/all_to_all | solution.py:97
  138.9 5.4 %gather_fusion.3 = bf16[1536,256]{1,0:T(8,128)(2,1)} fusion(bf16[1536,256]{1,0:T(8,128)(2,1)S(1)} %bitcast.126, s32[2048]{0:T(1024)S(1)} %pad_clamp_fusion), kind=kCustom, calls=%fused_computation.1.clone | custom fusion | bytes 1579008 | tf_op jit(solution)/shard_map/jit(_take)/gather | solution.py:107
  144.3 2.9 %fusion.1 = f32[1536,256]{1,0:T(8,128)S(1)} fusion(f32[4,1536]{1,0:T(4,128)S(1)} %copy-done.12, bf16[1536,256]{1,0:T(8,128)(2,1)} %gather_fusion.3, f32[256]{0:T(256)S(1)} %bitcast.145, pred[1536]{0:T(1024)(128)(4,1)S(1)} %get-tuple-element.22, f32[3,4,256]{2,1,0:T(4,128)S(1)} %copy-done.14), kind=kOutput, calls=%fused_computation.11 | convolution fusion | flops 20447232 | bytes 2391040 | tf_op jit(solution)/shard_map/ce,ch->eh/dot_general | solution.py:22
  152.1 6.1 %reduce-scatter.6.cloned.1.call-done = f32[384,256]{1,0:T(8,128)} async-done(((f32[768,256]{1,0:T(8,128)}), f32[384,256]{1,0:T(8,128)}) %reduce-scatter.6.cloned.1.call-update) | async-done | bytes 393232 | tf_op jit(solution)/shard_map/reduce_scatter | solution.py:117
  159.3 7.8 %all_gather.31 = bf16[384,512]{1,0:T(8,128)(2,1)S(1)} all-gather(bf16[384,256]{1,0:T(8,128)(2,1)S(1)} %multiply_convert_fusion.1), channel_id=1, replica_groups=mesh['groups'=2,'dom'=4,'feat'=2,'sub'=2] {'feat'}, dimensions={1}, use_global_device_ids=true | all-gather | bytes 589824 | tf_op jit(solution)/shard_map/all_gather | solution.py:125
  168.4 4.9 %all-reduce.1 = (f32[384]{0:T(512)S(1)}, f32[384]{0:T(512)S(1)}) all-reduce(f32[384]{0:T(512)S(1)} %get-tuple-element.11, f32[384]{0:T(512)S(1)} %get-tuple-element.10), channel_id=1, replica_groups=mesh['groups'=2,'dom'=4,'feat'=2,'sub'=2] {'feat'}, use_global_device_ids=true, to_apply=%region_9.13 | all-reduce | flops 768 | bytes 6144 | tf_op jit(solution)/shard_map/psum | solution.py:129
  176.3 11.8 %all_gather.33 = bf16[768,512]{0,1:T(8,128)(2,1)S(1)} all-gather(bf16[768,256]{0,1:T(8,128)(2,1)S(1)} %all_gather.32), channel_id=1, replica_groups=mesh['groups'=2,'dom'=4,'feat'=2,'sub'=2] {'feat'}, dimensions={1}, use_global_device_ids=true | all-gather | bytes 1179648 | tf_op jit(solution)/shard_map/all_gather | solution.py:14
  191.0 4.8 %all-to-all-start.2 = ((bf16[4,3,64,256]{3,2,1,0:T(8,128)(2,1)}), bf16[4,3,64,256]{3,2,1,0:T(8,128)(2,1)}, u32[]{:S(2)}, u32[]{:S(2)}) async-start(bf16[4,3,64,256]{3,2,1,0:T(8,128)(2,1)} %broadcast_select_fusion), calls=%async_computation.4 | async-start | bytes 786432 | tf_op jit(solution)/shard_map/all_to_all | solution.py:97
  198.1 9.0 %all-to-all-done.2 = bf16[4,3,64,256]{3,2,1,0:T(8,128)(2,1)} async-done(((bf16[4,3,64,256]{3,2,1,0:T(8,128)(2,1)}), bf16[4,3,64,256]{3,2,1,0:T(8,128)(2,1)}, u32[]{:S(2)}, u32[]{:S(2)}) %all-to-all-start.2) | async-done | bytes 393248 | tf_op jit(solution)/shard_map/all_to_all | solution.py:97
  208.3 5.4 %gather_fusion.6 = bf16[1536,256]{1,0:T(8,128)(2,1)} fusion(bf16[1536,256]{1,0:T(8,128)(2,1)S(1)} %bitcast.125, s32[2048]{0:T(1024)S(1)} %pad_clamp_fusion), kind=kCustom, calls=%fused_computation.4.clone | custom fusion | bytes 1579008 | tf_op jit(solution)/shard_map/jit(_take)/gather | solution.py:107
  213.6 2.9 %fusion = f32[1536,256]{1,0:T(8,128)S(1)} fusion(f32[4,1536]{1,0:T(4,128)S(1)} %copy-done.12, bf16[1536,256]{1,0:T(8,128)(2,1)} %gather_fusion.6, f32[256]{0:T(256)S(1)} %bitcast.144, pred[1536]{0:T(1024)(128)(4,1)S(1)} %get-tuple-element.22, f32[3,4,256]{2,1,0:T(4,128)S(1)} %copy-done.14), kind=kOutput, calls=%fused_computation.9 | convolution fusion | flops 20447232 | bytes 2391040 | tf_op jit(solution)/shard_map/ce,ch->eh/dot_general | solution.py:22
  221.5 6.1 %reduce-scatter.8.cloned.1.call-done = f32[384,256]{1,0:T(8,128)} async-done(((f32[768,256]{1,0:T(8,128)}), f32[384,256]{1,0:T(8,128)}) %reduce-scatter.8.cloned.1.call-update) | async-done | bytes 393232 | tf_op jit(solution)/shard_map/reduce_scatter | solution.py:117
  228.7 7.8 %all_gather.34 = bf16[384,512]{1,0:T(8,128)(2,1)S(1)} all-gather(bf16[384,256]{1,0:T(8,128)(2,1)S(1)} %multiply_convert_fusion), channel_id=1, replica_groups=mesh['groups'=2,'dom'=4,'feat'=2,'sub'=2] {'feat'}, dimensions={1}, use_global_device_ids=true | all-gather | bytes 589824 | tf_op jit(solution)/shard_map/all_gather | solution.py:125
  237.8 4.9 %all-reduce = (f32[384]{0:T(512)S(1)}, f32[384]{0:T(512)S(1)}) all-reduce(f32[384]{0:T(512)S(1)} %get-tuple-element.8, f32[384]{0:T(512)S(1)} %get-tuple-element.6), channel_id=1, replica_groups=mesh['groups'=2,'dom'=4,'feat'=2,'sub'=2] {'feat'}, use_global_device_ids=true, to_apply=%region_14.18 | all-reduce | flops 768 | bytes 6144 | tf_op jit(solution)/shard_map/psum | solution.py:129
  (121 shorter events, 52.7 us)
Async XLA Ops:
  6.5 66.9 %copy-start = (f32[4,2048]{1,0:T(4,128)S(1)}, f32[4,2048]{1,0:T(4,128)}, u32[]{:S(2)}) copy-start(f32[4,2048]{1,0:T(4,128)} %param.27) | copy-start | bytes 98308
  6.5 6.5 %copy-start.20 = (s32[2,32]{1,0:T(2,128)S(1)}, s32[2,32]{1,0:T(2,128)}, u32[]{:S(2)}) copy-start(s32[2,32]{1,0:T(2,128)} %param.25) | copy-start | bytes 772
  6.5 6.6 %copy-start.11 = (bf16[768,256]{1,0:T(8,128)(2,1)S(1)}, bf16[768,256]{1,0:T(8,128)(2,1)}, u32[]{:S(2)}) copy-start(bf16[768,256]{1,0:T(8,128)(2,1)} %param.24) | copy-start | bytes 1179652
  6.5 6.8 %copy-start.19 = (s32[1,4,3]{1,0,2:T(1,128)S(1)}, s32[1,4,3]{1,0,2:T(1,128)}, u32[]{:S(2)}) copy-start(s32[1,4,3]{1,0,2:T(1,128)} %param.28) | copy-start | bytes 148
  6.5 54.7 %all-to-all-start = ((bf16[4,512,512]{2,1,0:T(8,128)(2,1)}), bf16[4,512,512]{2,1,0:T(8,128)(2,1)S(1)}, u32[]{:S(2)}, u32[]{:S(2)}) async-start(bf16[4,512,512]{2,1,0:T(8,128)(2,1)} %bitcast.137), calls=%async_computation | async-start | bytes 4194304 | tf_op jit(solution)/shard_map/all_to_all | solution.py:63
  13.0 75.8 %reduce-scatter.4.cloned.1.call-start = ((), (), s32[]{:S(2)}) async-start(), calls=%async_computation.6 | async-start | bytes 1179648 | tf_op jit(solution)/shard_map/reduce_scatter | solution.py:117
  27.0 2.1 copy-start.16
  27.0 2.1 copy-start.13
  64.8 8.6 %copy-start.14 = (f32[3,4,256]{2,1,0:T(4,128)S(1)}, f32[3,4,256]{2,1,0:T(4,128)}, u32[]{:S(2)}) copy-start(f32[3,4,256]{2,1,0:T(4,128)} %param.35) | copy-start | bytes 36868
  73.4 3.7 %copy-start.2 = (f32[32,64,256]{2,1,0:T(8,128)S(1)}, f32[32,64,256]{2,1,0:T(8,128)}, u32[]{:S(2)}) copy-start(f32[32,64,256]{2,1,0:T(8,128)} %gather_fusion.1) | copy-start | bytes 6291460
  79.9 1.4 copy-start.21
  79.9 1.6 copy-start.17
  79.9 1.6 copy-start.18
  79.9 1.7 copy-start.4
  120.1 6.4 %copy-start.9 = (bf16[768,256]{1,0:T(8,128)(2,1)}, bf16[768,256]{1,0:T(8,128)(2,1)S(1)}, u32[]{:S(2)}) copy-start(bf16[768,256]{1,0:T(8,128)(2,1)S(1)} %convolution_convert_fusion.1) | copy-start | bytes 1179652
  120.2 6.3 %copy-start.15 = (s32[1536]{0:T(1024)S(1)}, s32[1536]{0:T(1024)}, u32[]{:S(2)}) copy-start(s32[1536]{0:T(1024)} %param.30) | copy-start | bytes 18436
  121.6 16.1 %all-to-all-start.1 = ((bf16[4,3,64,256]{3,2,1,0:T(8,128)(2,1)}), bf16[4,3,64,256]{3,2,1,0:T(8,128)(2,1)}, u32[]{:S(2)}, u32[]{:S(2)}) async-start(bf16[4,3,64,256]{3,2,1,0:T(8,128)(2,1)} %broadcast_select_fusion.1), calls=%async_computation.2 | async-start | bytes 786432 | tf_op jit(solution)/shard_map/all_to_all | solution.py:97
  126.5 31.7 %reduce-scatter.6.cloned.1.call-start = ((), (), s32[]{:S(2)}) async-start(), calls=%async_computation.7 | async-start | bytes 1179648 | tf_op jit(solution)/shard_map/reduce_scatter | solution.py:117
  138.9 5.4 %copy-start.12 = (f32[4,1536]{1,0:T(4,128)S(1)}, f32[4,1536]{1,0:T(4,128)}, u32[]{:S(2)}) copy-start(f32[4,1536]{1,0:T(4,128)} %param.31) | copy-start | bytes 73732
  152.1 21.2 %copy-start.8 = (bf16[768,256]{0,1:T(8,128)(2,1)S(1)}, bf16[768,256]{0,1:T(8,128)(2,1)}, u32[]{:S(2)}) copy-start(bf16[768,256]{0,1:T(8,128)(2,1)} %copy-done.7) | copy-start | bytes 1179652
  189.5 6.3 %copy-start.10 = (bf16[768,256]{1,0:T(8,128)(2,1)}, bf16[768,256]{1,0:T(8,128)(2,1)S(1)}, u32[]{:S(2)}) copy-start(bf16[768,256]{1,0:T(8,128)(2,1)S(1)} %convolution_convert_fusion) | copy-start | bytes 1179652
  191.0 16.1 %all-to-all-start.2 = ((bf16[4,3,64,256]{3,2,1,0:T(8,128)(2,1)}), bf16[4,3,64,256]{3,2,1,0:T(8,128)(2,1)}, u32[]{:S(2)}, u32[]{:S(2)}) async-start(bf16[4,3,64,256]{3,2,1,0:T(8,128)(2,1)} %broadcast_select_fusion), calls=%async_computation.4 | async-start | bytes 786432 | tf_op jit(solution)/shard_map/all_to_all | solution.py:97
  195.8 31.7 %reduce-scatter.8.cloned.1.call-start = ((), (), s32[]{:S(2)}) async-start(), calls=%async_computation.8 | async-start | bytes 1179648 | tf_op jit(solution)/shard_map/reduce_scatter | solution.py:117
  221.5 21.2 %copy-start.6 = (bf16[768,256]{0,1:T(8,128)(2,1)S(1)}, bf16[768,256]{0,1:T(8,128)(2,1)}, u32[]{:S(2)}) copy-start(bf16[768,256]{0,1:T(8,128)(2,1)} %copy-done.5) | copy-start | bytes 1179652
  (4 other events, 3.7 us)
Sparse Core Ops, SparseCore 0:
  81.4 7.3 reduce-scatter.3
  150.9 7.2 reduce-scatter.5
  220.2 7.2 reduce-scatter.7
where the time goes:
time: 253 us; the launch traced here: 252 us
  blocking collectives  79.3 us (31%)
  waiting for transfers between devices  68.1 us (27%)
  local copies, waits for them, and re-layouts  33.8 us (13%)
  matrix products  31.6 us (12%)
  starting transfers between devices  16.2 us (6%)
  between operations  13.6 us (5%)
  other arithmetic  9.81 us (4%)
    all_gather x3, blocking collectives, widen_latent(): portion = lax.all_gather(latent, 'feat', axis=1, tiled=True)  34.9 us
    all_to_all x1, waiting for transfers between devices, local(): lax.all_to_all(grid_latent.reshape(partitions, band_share, model_width),...  32.1 us
    all_gather x3, blocking collectives, local(): lax.all_gather(hidden, 'feat', axis=1, tiled=True)  23.3 us
    gather x3, local copies, waits for them, and re-layouts, local(): gathered_rows = jnp.take(sender_table, source_rows, axis=0)  19.3 us
    reduce_scatter x3, waiting for transfers between devices, local(): lax.psum_scatter(partial_value, 'sub', scatter_dimension=0, tiled=True)  18.1 us
    all_to_all x2, waiting for transfers between devices, local(): lax.all_to_all(outgoing, 'dom', split_axis=0, concat_axis=0, tiled=True)  17.9 us
    psum x3, blocking collectives, local(): lax.psum((jnp.sum(update, axis=1), jnp.sum(update * update, axis=1)), 'fe...  14.8 us
    dot_general x8, matrix products, widen_latent(): jnp.dot(portion, weight, preferred_element_type=jnp.float32)  10.7 us
  transfers between devices with their start and end apart: 6, of which 6 were waited for; matrix products, arithmetic and copies ran while one was open for 5% of the time, Pallas kernels for 0%

commit v1 on v0

v1 whole, which is shorter than its diff:
```python
import functools

import jax
import jax.numpy as jnp
from jax import lax
from jax.experimental import pallas as pl
from jax.experimental.pallas import tpu as pltpu
from jax.sharding import PartitionSpec as P

TILE = 64
LAYERS = 3
CAP = 3
EPSILON = 1e-05
DEVICE_MESH = pl.DeviceIdType.MESH
F32 = jnp.float32
BF16 = jnp.bfloat16


def silu(value):
    half = 0.5 * value
    return half + half * jnp.tanh(half)


def contract_rows(left, right, precision=None):
    return lax.dot_general(
        left, right, (((0,), (0,)), ((), ())), preferred_element_type=F32, precision=precision
    )


def plan_kernel(n_dom, tile_count, encoder_tiles, mesh_tiles, halo_tiles, plan, last):
    dom = lax.axis_index("dom")
    previous = lax.rem(dom + n_dom - 1, n_dom)
    following = lax.rem(dom + 1, n_dom)

    def chain(tiles, row):
        blocks = tiles.shape[1]

        def clear(t, carry):
            last[t] = blocks
            return carry

        def follow(block, carry):
            target = tiles[1, block]
            plan[row + 1, block] = last[target]
            plan[row + 3, block] = target
            last[target] = block
            return carry

        def keep(t, carry):
            plan[row + 2, t] = last[t]
            return carry

        lax.fori_loop(0, tile_count, clear, 0)
        lax.fori_loop(0, blocks, follow, 0)
        lax.fori_loop(0, tile_count, keep, 0)

    def grid_place(block, carry):
        plan[0, block] = encoder_tiles[0, block]
        return carry

    def mesh_place(block, carry):
        tile = mesh_tiles[0, block]
        beyond = jnp.maximum(tile - tile_count, 0)
        owner = lax.div(beyond, CAP)
        slot = lax.rem(beyond, CAP)
        way = jnp.where(owner == previous, 0, jnp.where(owner == following, 1, 2))
        plan[4, block] = jnp.where(tile < tile_count, tile, tile_count + CAP * way + slot)
        return carry

    lax.fori_loop(0, encoder_tiles.shape[1], grid_place, 0)
    lax.fori_loop(0, mesh_tiles.shape[1], mesh_place, 0)
    chain(encoder_tiles, 0)
    chain(mesh_tiles, 4)
    for way, step in enumerate((1, n_dom - 1, n_dom // 2)):
        peer = lax.rem(dom + step, n_dom)
        for slot in range(CAP):
            plan[8, CAP * way + slot] = jnp.maximum(halo_tiles[0, peer, slot], 0)


def kernel(
    sizes,
    plan,
    encoder_lanes,
    mesh_lanes,
    encoder_geometry,
    mesh_geometry,
    edge_weight,
    edge_bias,
    node_bias,
    grid_latent,
    mesh_latent,
    sender_weight,
    receiver_weight,
    node_weight,
    output_weight,
    norm_gain,
    out,
    grid_half,
    sender_w,
    receiver_w,
    node_w,
    output_w,
    gain,
    grid_out,
    grid_table,
    latents,
    first_table,
    second_table,
    local_table,
    halo_out,
    receivers,
    base,
    terms_enc,
    terms_mesh,
    sums,
    share_out,
    share_in,
    hidden,
    fetch_sem,
    send_sem,
    recv_sem,
):
    n_dom, n_feat = sizes
    dom = lax.axis_index("dom")
    feat = lax.axis_index("feat")
    sub = lax.axis_index("sub")
    width = base.shape[2]
    mesh_rows = latents.shape[2]
    tile_count = mesh_rows // TILE
    half_tiles = tile_count // 2
    half_rows = mesh_rows // 2
    part_rows = half_rows // n_feat
    half_band = grid_half.shape[1]
    model_width = grid_half.shape[2]
    half_model = model_width // 2
    half_tile = TILE // 2
    half_units = half_band // half_tile

    tables = (first_table, second_table)
    fetches = []
    sends = []

    def fetch(source, target):
        copy = pltpu.make_async_copy(source, target, fetch_sem.at[len(fetches)])
        copy.start()
        fetches.append(copy)
        return copy

    def send(source, target, device):
        slot = len(sends)
        copy = pltpu.make_async_remote_copy(
            src_ref=source,
            dst_ref=target,
            send_sem=send_sem.at[slot],
            recv_sem=recv_sem.at[slot],
            device_id=device,
            device_id_type=DEVICE_MESH,
        )
        copy.start()
        sends.append(copy)
        return copy

    sibling = {"sub": 1 - sub}
    own_rows = pl.ds(pl.multiple_of(sub * half_rows, half_rows), half_rows)

    got_grid = fetch(
        grid_latent.at[:, pl.ds(pl.multiple_of(sub * half_band, half_band), half_band), :], grid_half
    )
    got_sender = fetch(sender_weight, sender_w)
    got_latent = fetch(mesh_latent, latents.at[0, feat])
    got_receiver = fetch(receiver_weight, receiver_w)
    got_node = fetch(node_weight, node_w)
    got_output = fetch(output_weight, output_w.at[feat])
    got_gain = fetch(norm_gain, gain.at[feat])

    barrier = pltpu.get_barrier_semaphore()
    dom_peers = [lax.rem(dom + step, n_dom) for step in range(1, n_dom)]
    feat_peers = [lax.rem(feat + step, n_feat) for step in range(1, n_feat)]
    feat_sources = [lax.rem(feat + n_feat - step, n_feat) for step in range(1, n_feat)]
    for peer in dom_peers:
        pl.semaphore_signal(barrier, inc=1, device_id={"dom": peer}, device_id_type=DEVICE_MESH)
    for peer in feat_peers:
        pl.semaphore_signal(barrier, inc=1, device_id={"feat": peer}, device_id_type=DEVICE_MESH)
    pl.semaphore_signal(barrier, inc=1, device_id=sibling, device_id_type=DEVICE_MESH)
    pl.semaphore_wait(barrier, n_dom + n_feat - 1)

    got_latent.wait()
    first_latents = [
        send(latents.at[0, feat, own_rows, :], latents.at[0, feat, own_rows, :], {"feat": peer})
        for peer in feat_peers
    ]

    got_grid.wait()
    got_sender.wait()

    def band_rows(source):
        return pl.ds(source * (2 * half_units) + sub * half_units, half_units)

    def project(peer):
        values = jnp.dot(grid_half[peer], sender_w[0], preferred_element_type=F32)
        return values.astype(BF16).reshape(half_units, half_tile, width)

    steps = sorted(range(1, n_dom), key=lambda step: -min(step, n_dom - step))
    grid_copies = []
    for step in steps:
        peer = lax.rem(dom + step, n_dom)
        grid_out[step - 1] = project(peer)
        grid_copies.append(
            send(grid_out.at[step - 1], grid_table.at[band_rows(dom)], {"dom": peer})
        )
    grid_table[band_rows(dom)] = project(dom)
    share_grid = [
        send(grid_table.at[band_rows(dom)], grid_table.at[band_rows(dom)], sibling)
    ]

    got_output.wait()
    got_gain.wait()
    model_half = pl.ds(pl.multiple_of(sub * half_model, half_model), half_model)
    weight_copies = []
    for layer in range(LAYERS):
        part = output_w.at[feat, layer, model_half, :]
        weight_copies.append([send(part, part, {"feat": peer}) for peer in feat_peers])
    gain_copies = [send(gain.at[feat], gain.at[feat], {"feat": peer}) for peer in feat_peers]

    def geometry_terms(geometry, layer, target):
        def body(pair, carry):
            rows = pl.ds(pl.multiple_of(pair * 2 * TILE, 2 * TILE), 2 * TILE)
            target[rows, :] = (
                contract_rows(geometry[:, rows], edge_weight[layer], lax.Precision.HIGHEST)
                + edge_bias[pl.ds(layer, 1), :]
            )
            return carry

        lax.fori_loop(0, target.shape[0] // (2 * TILE), body, 0)

    geometry_terms(encoder_geometry, 0, terms_enc)

    share_first = []
    for source, copy in zip(feat_sources, first_latents):
        copy.wait_recv()
        part = latents.at[0, source, own_rows, :]
        share_first.append(send(part, part, sibling))

    for layer in range(1, LAYERS):
        geometry_terms(mesh_geometry, layer, terms_mesh.at[layer - 1])

    got_receiver.wait()
    got_node.wait()
    for copy in share_first:
        copy.wait_recv()

    def whole(layer, rows):
        return jnp.concatenate([latents[layer, f, rows, :] for f in range(n_feat)], axis=1)

    def widen(layer):
        base[0] = jnp.dot(whole(layer, own_rows), node_w[layer], preferred_element_type=F32)
        receivers[...] = jnp.dot(
            whole(layer, slice(None)), receiver_w[layer], preferred_element_type=F32
        ).reshape(receivers.shape)

    widen(0)

    for step, copy in zip(steps, grid_copies):
        copy.wait_recv()
        source = lax.rem(dom + n_dom - step, n_dom)
        part = grid_table.at[band_rows(source)]
        share_grid.append(send(part, part, sibling))
    for copy in share_grid:
        copy.wait_recv()

    def edge_sums(lanes, terms, load, row):
        blocks = 2 * lanes.shape[0]
        zero_slot = blocks
        sums[zero_slot] = jnp.zeros((TILE, width), F32)
        lane_at = lax.broadcasted_iota(jnp.int32, (1, 2 * TILE), 1)
        shift = jnp.where(lane_at >= TILE, TILE, 0)
        row_at = lax.broadcasted_iota(jnp.int32, (2 * TILE, 2 * TILE), 0)

        def body(pair, carry):
            rows = pl.ds(pl.multiple_of(pair * 2 * TILE, 2 * TILE), 2 * TILE)
            wanted = lanes[pl.ds(pair, 1), :] + shift
            chosen = jnp.where(row_at == wanted, 1.0, 0.0).astype(BF16)
            source = jnp.concatenate(
                [load(plan[row, 2 * pair]), load(plan[row, 2 * pair + 1])], axis=0
            )
            before = contract_rows(chosen, source) + terms[rows, :]
            for side in range(2):
                block = 2 * pair + side
                message = silu(
                    before[side * TILE : (side + 1) * TILE] + receivers[plan[row + 3, block]]
                )
                sums[block] = message + sums[plan[row + 1, block]]
            return carry

        lax.fori_loop(0, blocks // 2, body, 0)

    def load_grid(tile):
        return jnp.concatenate([grid_table[2 * tile], grid_table[2 * tile + 1]], axis=0)

    for layer in range(LAYERS):
        if layer == 0:
            edge_sums(encoder_lanes, terms_enc, load_grid, 0)
        else:
            senders = (
                jnp.dot(whole(layer, slice(None)), sender_w[layer], preferred_element_type=F32)
                .astype(BF16)
                .reshape(tile_count, TILE, width)
            )
            local_table[...] = senders
            tables[layer - 1][:tile_count] = senders
            table = tables[layer - 1]
            half = pl.ds(pl.multiple_of(sub * half_tile, half_tile), half_tile)
            halo_copies = []
            for way, step in enumerate((1, n_dom - 1, n_dom // 2)):
                peer = lax.rem(dom + step, n_dom)
                for slot in range(CAP):
                    listed = local_table[plan[8, CAP * way + slot]]
                    halo_out[layer - 1, way, slot] = jnp.where(
                        sub == 0, listed[:half_tile], listed[half_tile:]
                    )
                halo_copies.append(
                    send(
                        halo_out.at[layer - 1, way],
                        table.at[pl.ds(tile_count + CAP * way, CAP), half, :],
                        {"dom": peer},
                    )
                )
            widen(layer)
            share_halo = []
            for way, copy in enumerate(halo_copies):
                copy.wait_recv()
                part = table.at[pl.ds(tile_count + CAP * way, CAP), half, :]
                share_halo.append(send(part, part, sibling))
            for copy in share_halo:
                copy.wait_recv()
            edge_sums(mesh_lanes, terms_mesh.at[layer - 1], lambda at: table[at], 4)

        ends = 2 if layer == 0 else 6
        for k in range(half_tiles):
            theirs = plan[ends, (1 - sub) * half_tiles + k]
            share_out[layer, k] = sums[theirs]
        sum_copy = send(share_out.at[layer], share_in.at[layer], sibling)
        for k in range(half_tiles):
            mine = plan[ends, sub * half_tiles + k]
            rows = slice(k * TILE, (k + 1) * TILE)
            base[0, rows, :] = base[0, rows, :] + sums[mine]
        if layer == 0:
            share_weights = []
            for at in range(LAYERS):
                share_weights.append([])
                for source, copy in zip(feat_sources, weight_copies[at]):
                    copy.wait_recv()
                    part = output_w.at[source, at, model_half, :]
                    share_weights[at].append(send(part, part, sibling))
            for copy in gain_copies:
                copy.wait_recv()
        sum_copy.wait_recv()
        active = silu(
            base[0]
            + share_in[layer].reshape(half_rows, width)
            + node_bias[pl.ds(layer, 1), :]
        ).astype(BF16)
        for f in range(n_feat):
            hidden[layer, 0, f] = active[f * part_rows : (f + 1) * part_rows]
        hidden_copies = [
            send(hidden.at[layer, 0, peer], hidden.at[layer, 1, feat], {"feat": peer})
            for peer in feat_peers
        ]
        hidden[layer, 1, feat] = hidden[layer, 0, feat]
        for copy in hidden_copies:
            copy.wait_recv()
        for copy in share_weights[layer]:
            copy.wait_recv()
        whole_hidden = jnp.concatenate([hidden[layer, 1, f] for f in range(n_feat)], axis=1)
        updates = [
            jnp.dot(whole_hidden, output_w[f, layer], preferred_element_type=F32)
            for f in range(n_feat)
        ]
        row_mean = sum(jnp.sum(u, axis=1, keepdims=True) for u in updates) / model_width
        row_squares = sum(jnp.sum(u * u, axis=1, keepdims=True) for u in updates) / model_width
        scale = lax.rsqrt(row_squares - row_mean * row_mean + EPSILON)
        def part_of(source):
            return pl.ds(
                pl.multiple_of(sub * half_rows + source * part_rows, part_rows), part_rows
            )

        mine = part_of(feat)
        for f in range(n_feat):
            normed = (updates[f] - row_mean) * scale * gain[f, pl.ds(layer, 1), :]
            latents[layer + 1, f, mine, :] = (
                latents[layer, f, mine, :].astype(F32) + normed
            ).astype(BF16)
        columns = (lambda device: pl.ds(0, n_feat)) if layer < LAYERS - 1 else (lambda device: device)
        latent_copies = [
            send(
                latents.at[layer + 1, columns(peer), mine, :],
                latents.at[layer + 1, columns(peer), mine, :],
                {"feat": peer},
            )
            for peer in feat_peers
        ]
        part = latents.at[layer + 1, columns(feat), mine, :]
        share_latent = [send(part, part, sibling)]
        for source, copy in zip(feat_sources, latent_copies):
            copy.wait_recv()
            part = latents.at[layer + 1, columns(feat), part_of(source), :]
            share_latent.append(send(part, part, sibling))
        for copy in share_latent:
            copy.wait_recv()

    out[...] = latents[LAYERS, feat]
    for copy in sends:
        copy.wait_send()


def local(
    n_dom,
    n_feat,
    grid_latent,
    mesh_latent,
    encoder_tiles,
    encoder_lanes,
    encoder_geometry,
    halo_tiles,
    mesh_tiles,
    mesh_lanes,
    mesh_geometry,
    sender_weight,
    receiver_weight,
    node_weight,
    edge_weight,
    edge_bias,
    node_bias,
    output_weight,
    norm_gain,
):
    model, width = sender_weight.shape[1:]
    grid_rows = grid_latent.shape[0]
    mesh_rows = mesh_latent.shape[0]
    tile_count = mesh_rows // TILE
    band = grid_rows // n_dom
    enc_edges = encoder_lanes.shape[0]
    mesh_edges = mesh_lanes.shape[0]
    half_rows = mesh_rows // 2
    part_rows = half_rows // n_feat
    copies = 2 * n_dom + 16 + (n_feat - 1) * (2 + 2 * LAYERS + 1 + 3 * LAYERS) + 2 * LAYERS
    copies += 6 * (LAYERS - 1)
    smem = pl.BlockSpec(memory_space=pltpu.SMEM)
    plan = pl.pallas_call(
        functools.partial(plan_kernel, n_dom, tile_count),
        out_shape=jax.ShapeDtypeStruct((9, max(enc_edges, mesh_edges) // TILE), jnp.int32),
        in_specs=[smem] * 3,
        out_specs=smem,
        scratch_shapes=[pltpu.SMEM((tile_count,), jnp.int32)],
    )(encoder_tiles, mesh_tiles, halo_tiles)
    vmem = pl.BlockSpec(memory_space=pltpu.VMEM)
    far = pl.BlockSpec(memory_space=pl.ANY)
    return pl.pallas_call(
        functools.partial(kernel, (n_dom, n_feat)),
        out_shape=jax.ShapeDtypeStruct((mesh_rows, width), BF16),
        in_specs=[smem] + [vmem] * 7 + [far] * 7,
        out_specs=vmem,
        scratch_shapes=[
            pltpu.VMEM((n_dom, band // 2, model), BF16),
            pltpu.VMEM((LAYERS, model, width), BF16),
            pltpu.VMEM((LAYERS, model, width), BF16),
            pltpu.VMEM((LAYERS, model, width), BF16),
            pltpu.VMEM((n_feat, LAYERS, model, width), BF16),
            pltpu.VMEM((n_feat, LAYERS, width), F32),
            pltpu.VMEM((n_dom - 1, band // TILE, TILE // 2, width), BF16),
            pltpu.VMEM((2 * grid_rows // TILE, TILE // 2, width), BF16),
            pltpu.VMEM((LAYERS + 1, n_feat, mesh_rows, width), BF16),
            pltpu.VMEM((tile_count + 3 * CAP, TILE, width), BF16),
            pltpu.VMEM((tile_count + 3 * CAP, TILE, width), BF16),
            pltpu.VMEM((tile_count, TILE, width), BF16),
            pltpu.VMEM((LAYERS - 1, 3, CAP, TILE // 2, width), BF16),
            pltpu.VMEM((tile_count, TILE, width), F32),
            pltpu.VMEM((1, half_rows, width), F32),
            pltpu.VMEM((enc_edges, width), F32),
            pltpu.VMEM((LAYERS - 1, mesh_edges, width), F32),
            pltpu.VMEM((max(enc_edges, mesh_edges) // TILE + 1, TILE, width), F32),
            pltpu.VMEM((LAYERS, tile_count // 2, TILE, width), F32),
            pltpu.VMEM((LAYERS, tile_count // 2, TILE, width), F32),
            pltpu.VMEM((LAYERS, 2, n_feat, part_rows, width), BF16),
            pltpu.SemaphoreType.DMA((8,)),
            pltpu.SemaphoreType.DMA((copies,)),
            pltpu.SemaphoreType.DMA((copies,)),
        ],
        compiler_params=pltpu.CompilerParams(
            collective_id=0, has_side_effects=True, vmem_limit_bytes=48 * 1024 * 1024
        ),
    )(
        plan,
        encoder_lanes.reshape(-1, 2 * TILE),
        mesh_lanes.reshape(-1, 2 * TILE),
        encoder_geometry,
        mesh_geometry,
        edge_weight,
        edge_bias,
        node_bias,
        grid_latent.reshape(n_dom, band, model),
        mesh_latent,
        sender_weight,
        receiver_weight,
        node_weight,
        output_weight,
        norm_gain,
    )


def solution(mesh):
    in_specs = (
        P(("groups", "dom"), None),
        P(("groups", "dom"), "feat"),
        P(None, ("dom", "sub")),
        P(("dom", "sub")),
        P(None, ("dom", "sub")),
        P("dom", None, None),
        P(None, ("dom", "sub")),
        P(("dom", "sub")),
        P(None, ("dom", "sub")),
        P(None, None, "feat"),
        P(None, None, "feat"),
        P(None, None, "feat"),
        P(None, None, "feat"),
        P(None, "feat"),
        P(None, "feat"),
        P(None, None, "feat"),
        P(None, "feat"),
    )
    out_specs = P(("groups", "dom"), "feat")
    return jax.shard_map(
        functools.partial(local, mesh.shape["dom"], mesh.shape["feat"]),
        mesh=mesh,
        in_specs=in_specs,
        out_specs=out_specs,
        check_vma=False,
    )
```

time: 253 us -> 101 us (0.40)
  Pallas kernels: 0 us -> 84.8 us
  blocking collectives: 79.3 us -> 0 us
  waiting for transfers between devices: 68.1 us -> 0 us
  matrix products: 31.6 us -> 0 us
  local copies, waits for them, and re-layouts: 33.8 us -> 15.5 us
  starting transfers between devices: 16.2 us -> 0 us
  between operations: 13.6 us -> 0.04 us
  other arithmetic: 9.81 us -> 0 us
    pallas_call x0 -> x2, Pallas kernels: none -> 84.8 us  [the longest x1 81.9 us: local(): pl.pallas_call(functools.partial(kernel, (n_dom, n_feat)), out_shape=jax....]
    all_gather x9 -> x0, blocking collectives: 64.5 us -> none  [the longest x3 34.9 us: widen_latent(): portion = lax.all_gather(latent, 'feat', axis=1, tiled=True)]
    all_to_all x3 -> x0, waiting for transfers between devices: 50 us -> none  [the longest x1 32.1 us: local(): lax.all_to_all(grid_latent.reshape(partitions, band_share, model_width),...]
    dot_general x18 -> x0, matrix products: 31.6 us -> none  [the longest x8 10.7 us: widen_latent(): jnp.dot(portion, weight, preferred_element_type=jnp.float32)]
    gather x8 -> x0, local copies, waits for them, and re-layouts: 23.7 us -> none  [the longest x3 19.3 us: local(): gathered_rows = jnp.take(sender_table, source_rows, axis=0)]
    reduce_scatter x3 -> x0, waiting for transfers between devices: 18.1 us -> none  [local(): lax.psum_scatter(partial_value, 'sub', scatter_dimension=0, tiled=True)]
    all_to_all x3 -> x0, starting transfers between devices: 16.2 us -> none  [the longest x2 9.73 us: local(): lax.all_to_all(outgoing, 'dom', split_axis=0, concat_axis=0, tiled=True)]
    psum x3 -> x0, blocking collectives: 14.8 us -> none  [local(): lax.psum((jnp.sum(update, axis=1), jnp.sum(update * update, axis=1)), 'fe...]
  transfers between devices with their start and end apart: 6 -> 0, of which waited for: 6 -> 0; matrix products, arithmetic and copies ran while one was open for 5% -> 0% of each run, Pallas kernels for 0% -> 0%
where the time goes in v1:
time: 101 us; the launch traced here: 100 us
  Pallas kernels  84.8 us (84%)
  local copies, waits for them, and re-layouts  15.5 us (15%)
    pallas_call x1, Pallas kernels, local(): pl.pallas_call(functools.partial(kernel, (n_dom, n_feat)), out_shape=jax....  81.9 us
    unnamed x32, local copies, waits for them, and re-layouts  15.5 us
    pallas_call x1, Pallas kernels, local(): pl.pallas_call(functools.partial(plan_kernel, n_dom, tile_count), out_sha...  2.88 us

profile of v1, /device:TPU:0, one launch (start us, length us, event | category | flops | bytes accessed | tf_op | source)
XLA Modules:
  0.0 100.4 jit_solution(15879633021661155147)
XLA Ops:
  0.0 1.3 %copy.18.halo_tiles = s32[1,4,3]{2,1,0:T(4,128)} copy(s32[1,4,3]{1,0,2:T(1,128)} %param.22) | data formatting | bytes 96 | tf_op args[5]
  1.3 2.9 %shard_map.163.plan = s32[9,32]{1,0:T(8,128)} custom-call(s32[2,32]{1,0:T(2,128)} %encoder_tiles.1, s32[2,24]{1,0:T(2,128)} %mesh_tiles.1, s32[1,4,3]{2,1,0:T(4,128)} %copy.18.halo_tiles), custom_call_target="tpu_custom_call" | custom-call | tf_op jit(solution)/shard_map/pallas_call | solution.py:449
  4.2 0.0 copy-start
  4.2 1.6 %copy-done = bf16[2048,512]{1,0:T(8,128)(2,1)S(1)} copy-done((bf16[2048,512]{1,0:T(8,128)(2,1)S(1)}, bf16[2048,512]{1,0:T(8,128)(2,1)}, u32[]{:S(2)}) %copy-start) | copy-done | bytes 2097176
  5.8 0.0 copy-start.1
  5.8 1.1 %copy-done.1 = bf16[3,512,256]{2,1,0:T(8,128)(2,1)S(1)} copy-done((bf16[3,512,256]{2,1,0:T(8,128)(2,1)S(1)}, bf16[3,512,256]{2,1,0:T(8,128)(2,1)}, u32[]{:S(2)}) %copy-start.1) | copy-done | bytes 786456
  6.9 0.0 copy-start.2
  7.0 1.1 %copy-done.2 = bf16[3,512,256]{2,1,0:T(8,128)(2,1)S(1)} copy-done((bf16[3,512,256]{2,1,0:T(8,128)(2,1)S(1)}, bf16[3,512,256]{2,1,0:T(8,128)(2,1)}, u32[]{:S(2)}) %copy-start.2) | copy-done | bytes 786456
  8.1 0.0 copy-start.3
  8.1 1.1 %copy-done.3 = bf16[3,512,256]{2,1,0:T(8,128)(2,1)S(1)} copy-done((bf16[3,512,256]{2,1,0:T(8,128)(2,1)S(1)}, bf16[3,512,256]{2,1,0:T(8,128)(2,1)}, u32[]{:S(2)}) %copy-start.3) | copy-done | bytes 786456
  9.2 0.0 copy-start.4
  9.2 1.1 %copy-done.4 = bf16[3,512,256]{2,1,0:T(8,128)(2,1)S(1)} copy-done((bf16[3,512,256]{2,1,0:T(8,128)(2,1)S(1)}, bf16[3,512,256]{2,1,0:T(8,128)(2,1)}, u32[]{:S(2)}) %copy-start.4) | copy-done | bytes 786456
  10.4 1.0 copy-done.5
  11.3 0.8 copy-done.6
  12.1 0.7 copy-done.7
  12.8 0.7 copy-done.8
  13.5 0.7 copy-done.9
  14.2 0.7 copy-done.10
  14.9 0.7 copy-done.11
  15.6 0.7 copy-done.12
  16.3 0.7 copy-done.13
  17.0 0.7 copy-done.14
  17.7 81.9 %shard_map.164 = bf16[768,256]{1,0:T(8,128)(2,1)S(1)} custom-call(s32[9,32]{1,0:T(8,128)S(1)} %copy-done.7, s32[16,128]{1,0:T(8,128)S(1)} %bitcast.4, s32[12,128]{1,0:T(8,128)S(1)} %bitcast.5, f32[4,2048]{1,0:T(4,128)S(1)} %copy-done.6, f32[4,1536]{1,0:T(4,128)S(1)} %copy-done.8, f32[3,4,256]{2,1,0:T(4,128)S(1)} %copy-done.9, f32[3,256]{1,0:T(4,128)S(1)} %copy-done.12, ...), custom_call_target="tpu_custom_call" | custom-call | tf_op jit(solution)/shard_map/pallas_call | solution.py:458
  99.7 0.7 copy.20
  (10 shorter events, 0.0 us)
Async XLA Ops:
  4.2 1.6 %copy-start = (bf16[2048,512]{1,0:T(8,128)(2,1)S(1)}, bf16[2048,512]{1,0:T(8,128)(2,1)}, u32[]{:S(2)}) copy-start(bf16[2048,512]{1,0:T(8,128)(2,1)} %param.17) | copy-start | bytes 6291460
  5.8 1.1 %copy-start.1 = (bf16[3,512,256]{2,1,0:T(8,128)(2,1)S(1)}, bf16[3,512,256]{2,1,0:T(8,128)(2,1)}, u32[]{:S(2)}) copy-start(bf16[3,512,256]{2,1,0:T(8,128)(2,1)} %sender_weight.1) | copy-start | bytes 2359300
  6.9 1.1 %copy-start.2 = (bf16[3,512,256]{2,1,0:T(8,128)(2,1)S(1)}, bf16[3,512,256]{2,1,0:T(8,128)(2,1)}, u32[]{:S(2)}) copy-start(bf16[3,512,256]{2,1,0:T(8,128)(2,1)} %receiver_weight.1) | copy-start | bytes 2359300
  8.1 1.1 %copy-start.3 = (bf16[3,512,256]{2,1,0:T(8,128)(2,1)S(1)}, bf16[3,512,256]{2,1,0:T(8,128)(2,1)}, u32[]{:S(2)}) copy-start(bf16[3,512,256]{2,1,0:T(8,128)(2,1)} %node_weight.1) | copy-start | bytes 2359300
  9.2 1.1 %copy-start.4 = (bf16[3,512,256]{2,1,0:T(8,128)(2,1)S(1)}, bf16[3,512,256]{2,1,0:T(8,128)(2,1)}, u32[]{:S(2)}) copy-start(bf16[3,512,256]{2,1,0:T(8,128)(2,1)} %output_weight.1) | copy-start | bytes 2359300
  10.3 1.0 copy-start.5
  11.3 0.8 copy-start.6
  12.1 0.7 copy-start.7
  12.8 0.7 copy-start.8
  13.5 0.7 copy-start.9
  14.2 0.7 copy-start.10
  14.9 0.7 copy-start.11
  15.6 0.7 copy-start.12
  16.3 0.7 copy-start.13
  17.0 0.7 copy-start.14

commit v2 on v1

--- a/solution.py
+++ b/solution.py
@@ -11,6 +11,7 @@
 LAYERS = 3
 CAP = 3
 EPSILON = 1e-05
+VMEM_GRANT = 63 * 1024 * 1024
 DEVICE_MESH = pl.DeviceIdType.MESH
 F32 = jnp.float32
 BF16 = jnp.bfloat16
@@ -80,13 +81,13 @@
 def kernel(
     sizes,
     plan,
-    encoder_lanes,
-    mesh_lanes,
-    encoder_geometry,
-    mesh_geometry,
-    edge_weight,
-    edge_bias,
-    node_bias,
+    far_encoder_lanes,
+    far_mesh_lanes,
+    far_encoder_geometry,
+    far_mesh_geometry,
+    far_edge_weight,
+    far_edge_bias,
+    far_node_bias,
     grid_latent,
     mesh_latent,
     sender_weight,
@@ -95,6 +96,13 @@
     output_weight,
     norm_gain,
     out,
+    encoder_lanes,
+    mesh_lanes,
+    encoder_geometry,
+    mesh_geometry,
+    edge_weight,
+    edge_bias,
+    node_bias,
     grid_half,
     sender_w,
     receiver_w,
@@ -172,6 +180,15 @@
     got_node = fetch(node_weight, node_w)
     got_output = fetch(output_weight, output_w.at[feat])
     got_gain = fetch(norm_gain, gain.at[feat])
+    got_rest = [
+        fetch(far_encoder_geometry, encoder_geometry),
+        fetch(far_edge_weight, edge_weight),
+        fetch(far_edge_bias, edge_bias),
+        fetch(far_mesh_geometry, mesh_geometry),
+        fetch(far_encoder_lanes, encoder_lanes),
+        fetch(far_mesh_lanes, mesh_lanes),
+        fetch(far_node_bias, node_bias),
+    ]
 
     barrier = pltpu.get_barrier_semaphore()
     dom_peers = [lax.rem(dom + step, n_dom) for step in range(1, n_dom)]
@@ -233,6 +250,8 @@
 
         lax.fori_loop(0, target.shape[0] // (2 * TILE), body, 0)
 
+    for copy in got_rest:
+        copy.wait()
     geometry_terms(encoder_geometry, 0, terms_enc)
 
     share_first = []
@@ -452,15 +471,23 @@
         in_specs=[smem] * 3,
         out_specs=smem,
         scratch_shapes=[pltpu.SMEM((tile_count,), jnp.int32)],
+        compiler_params=pltpu.CompilerParams(vmem_limit_bytes=VMEM_GRANT),
     )(encoder_tiles, mesh_tiles, halo_tiles)
     vmem = pl.BlockSpec(memory_space=pltpu.VMEM)
-    far = pl.BlockSpec(memory_space=pl.ANY)
+    far = pl.BlockSpec(memory_space=pltpu.HBM)
     return pl.pallas_call(
         functools.partial(kernel, (n_dom, n_feat)),
         out_shape=jax.ShapeDtypeStruct((mesh_rows, width), BF16),
-        in_specs=[smem] + [vmem] * 7 + [far] * 7,
+        in_specs=[smem] + [far] * 14,
         out_specs=vmem,
         scratch_shapes=[
+            pltpu.VMEM((enc_edges // (2 * TILE), 2 * TILE), jnp.int32),
+            pltpu.VMEM((mesh_edges // (2 * TILE), 2 * TILE), jnp.int32),
+            pltpu.VMEM(encoder_geometry.shape, F32),
+            pltpu.VMEM(mesh_geometry.shape, F32),
+            pltpu.VMEM(edge_weight.shape, F32),
+            pltpu.VMEM(edge_bias.shape, F32),
+            pltpu.VMEM(node_bias.shape, F32),
             pltpu.VMEM((n_dom, band // 2, model), BF16),
             pltpu.VMEM((LAYERS, model, width), BF16),
             pltpu.VMEM((LAYERS, model, width), BF16),
@@ -482,12 +509,12 @@
             pltpu.VMEM((LAYERS, tile_count // 2, TILE, width), F32),
             pltpu.VMEM((LAYERS, tile_count // 2, TILE, width), F32),
             pltpu.VMEM((LAYERS, 2, n_feat, part_rows, width), BF16),
-            pltpu.SemaphoreType.DMA((8,)),
+            pltpu.SemaphoreType.DMA((14,)),
             pltpu.SemaphoreType.DMA((copies,)),
             pltpu.SemaphoreType.DMA((copies,)),
         ],
         compiler_params=pltpu.CompilerParams(
-            collective_id=0, has_side_effects=True, vmem_limit_bytes=48 * 1024 * 1024
+            collective_id=0, has_side_effects=True, vmem_limit_bytes=VMEM_GRANT
         ),
     )(
         plan,

time: 101 us -> 88.6 us (0.88)
  local copies, waits for them, and re-layouts: 15.5 us -> 3.12 us
    unnamed x32 -> x2, local copies, waits for them, and re-layouts: 15.5 us -> 3.12 us
where the time goes in v2:
time: 88.6 us; the launch traced here: 88.4 us
  Pallas kernels  85.2 us (96%)
  local copies, waits for them, and re-layouts  3.12 us (4%)
    pallas_call x1, Pallas kernels, local(): pl.pallas_call(functools.partial(kernel, (n_dom, n_feat)), out_shape=jax....  82.3 us
    unnamed x2, local copies, waits for them, and re-layouts  3.12 us
    pallas_call x1, Pallas kernels, local(): pl.pallas_call(functools.partial(plan_kernel, n_dom, tile_count), out_sha...  2.88 us

profile of v2, /device:TPU:0, one launch (start us, length us, event | category | flops | bytes accessed | tf_op | source)
XLA Modules:
  0.0 88.4 jit_solution(13370582321789868471)
XLA Ops:
  0.0 1.4 %copy.18.halo_tiles = s32[1,4,3]{2,1,0:T(4,128)} copy(s32[1,4,3]{1,0,2:T(1,128)} %param.22) | data formatting | bytes 96 | tf_op args[5]
  1.4 2.9 %shard_map.163.plan = s32[9,32]{1,0:T(8,128)} custom-call(s32[2,32]{1,0:T(2,128)} %encoder_tiles.1, s32[2,24]{1,0:T(2,128)} %mesh_tiles.1, s32[1,4,3]{2,1,0:T(4,128)} %copy.18.halo_tiles), custom_call_target="tpu_custom_call" | custom-call | tf_op jit(solution)/shard_map/pallas_call | solution.py:468
  4.2 82.3 %shard_map.164 = bf16[768,256]{1,0:T(8,128)(2,1)} custom-call(s32[9,32]{1,0:T(8,128)} %shard_map.163.plan, s32[16,128]{1,0:T(8,128)} %bitcast.4, s32[12,128]{1,0:T(8,128)} %bitcast.5, f32[4,2048]{1,0:T(4,128)} %far_encoder_geometry.1, f32[4,1536]{1,0:T(4,128)} %far_mesh_geometry.1, f32[3,4,256]{2,1,0:T(4,128)} %far_edge_weight.1, f32[3,256]{1,0:T(4,128)} %far_edge_bias.1, ...), custom_call_target="tpu_custom_call" | custom-call | tf_op jit(solution)/shard_map/pallas_call | solution.py:478
  86.6 1.8 %copy.20 = bf16[768,256]{1,0:T(8,128)(2,1)} copy(bf16[768,256]{1,0:T(8,128)(2,1)} %shard_map.164) | data formatting | bytes 786432

commit v3 on v2

--- a/solution.py
+++ b/solution.py
@@ -10,6 +10,8 @@
 TILE = 64
 LAYERS = 3
 CAP = 3
+CHUNK = 2
+SPLIT_ROWS = 32
 EPSILON = 1e-05
 VMEM_GRANT = 63 * 1024 * 1024
 DEVICE_MESH = pl.DeviceIdType.MESH
@@ -22,9 +24,9 @@
     return half + half * jnp.tanh(half)
 
 
-def contract_rows(left, right, precision=None):
+def contract_rows(left, right):
     return lax.dot_general(
-        left, right, (((0,), (0,)), ((), ())), preferred_element_type=F32, precision=precision
+        left, right, (((0,), (0,)), ((), ())), preferred_element_type=F32
     )
 
 
@@ -75,7 +77,7 @@
     for way, step in enumerate((1, n_dom - 1, n_dom // 2)):
         peer = lax.rem(dom + step, n_dom)
         for slot in range(CAP):
-            plan[8, CAP * way + slot] = jnp.maximum(halo_tiles[0, peer, slot], 0)
+            plan[8, CAP * way + slot] = jnp.maximum(halo_tiles[slot, 0, peer], 0)
 
 
 def kernel(
@@ -120,6 +122,7 @@
     base,
     terms_enc,
     terms_mesh,
+    split_weight,
     sums,
     share_out,
     share_in,
@@ -137,7 +140,8 @@
     tile_count = mesh_rows // TILE
     half_tiles = tile_count // 2
     half_rows = mesh_rows // 2
-    part_rows = half_rows // n_feat
+    chunks = half_tiles // CHUNK
+    chunk_rows = CHUNK * TILE
     half_band = grid_half.shape[1]
     model_width = grid_half.shape[2]
     half_model = model_width // 2
@@ -239,29 +243,35 @@
         weight_copies.append([send(part, part, {"feat": peer}) for peer in feat_peers])
     gain_copies = [send(gain.at[feat], gain.at[feat], {"feat": peer}) for peer in feat_peers]
 
-    def geometry_terms(geometry, layer, target):
-        def body(pair, carry):
-            rows = pl.ds(pl.multiple_of(pair * 2 * TILE, 2 * TILE), 2 * TILE)
-            target[rows, :] = (
-                contract_rows(geometry[:, rows], edge_weight[layer], lax.Precision.HIGHEST)
-                + edge_bias[pl.ds(layer, 1), :]
-            )
-            return carry
-
-        lax.fori_loop(0, target.shape[0] // (2 * TILE), body, 0)
+    def pieces(value):
+        high = value.astype(BF16).astype(F32)
+        middle = (value - high).astype(BF16).astype(F32)
+        return high, middle, value - high - middle
+
+    def split_geometry(geometry, target):
+        high, middle, low = pieces(geometry[...])
+        ones = jnp.ones((4, high.shape[1]), F32)
+        target[...] = jnp.concatenate(
+            [high, high, middle, middle, high, low, ones, 0.0 * ones], axis=0
+        ).astype(BF16)
 
     for copy in got_rest:
         copy.wait()
-    geometry_terms(encoder_geometry, 0, terms_enc)
+    split_geometry(encoder_geometry, terms_enc)
+    split_geometry(mesh_geometry, terms_mesh)
+    for layer in range(LAYERS):
+        high, middle, low = pieces(edge_weight[layer])
+        bias = pieces(edge_bias[pl.ds(layer, 1), :])
+        zeros = jnp.zeros((5, width), F32)
+        split_weight[layer] = jnp.concatenate(
+            [high, middle, high, middle, low, high, *bias, zeros], axis=0
+        ).astype(BF16)
 
     share_first = []
     for source, copy in zip(feat_sources, first_latents):
         copy.wait_recv()
         part = latents.at[0, source, own_rows, :]
         share_first.append(send(part, part, sibling))
-
-    for layer in range(1, LAYERS):
-        geometry_terms(mesh_geometry, layer, terms_mesh.at[layer - 1])
 
     got_receiver.wait()
     got_node.wait()
@@ -287,7 +297,7 @@
     for copy in share_grid:
         copy.wait_recv()
 
-    def edge_sums(lanes, terms, load, row):
+    def edge_sums(layer, lanes, terms, load, row):
         blocks = 2 * lanes.shape[0]
         zero_slot = blocks
         sums[zero_slot] = jnp.zeros((TILE, width), F32)
@@ -300,9 +310,10 @@
             wanted = lanes[pl.ds(pair, 1), :] + shift
             chosen = jnp.where(row_at == wanted, 1.0, 0.0).astype(BF16)
             source = jnp.concatenate(
-                [load(plan[row, 2 * pair]), load(plan[row, 2 * pair + 1])], axis=0
+                [load(plan[row, 2 * pair]), load(plan[row, 2 * pair + 1]), split_weight[layer]],
+                axis=0,
             )
-            before = contract_rows(chosen, source) + terms[rows, :]
+            before = contract_rows(jnp.concatenate([chosen, terms[:, rows]], axis=0), source)
             for side in range(2):
                 block = 2 * pair + side
                 message = silu(
@@ -311,14 +322,14 @@
                 sums[block] = message + sums[plan[row + 1, block]]
             return carry
 
-        lax.fori_loop(0, blocks // 2, body, 0)
+        lax.fori_loop(0, blocks // 2, body, 0, unroll=4)
 
     def load_grid(tile):
         return jnp.concatenate([grid_table[2 * tile], grid_table[2 * tile + 1]], axis=0)
 
     for layer in range(LAYERS):
         if layer == 0:
-            edge_sums(encoder_lanes, terms_enc, load_grid, 0)
+            edge_sums(0, encoder_lanes, terms_enc, load_grid, 0)
         else:
             senders = (
                 jnp.dot(whole(layer, slice(None)), sender_w[layer], preferred_element_type=F32)
@@ -352,17 +363,30 @@
                 share_halo.append(send(part, part, sibling))
             for copy in share_halo:
                 copy.wait_recv()
-            edge_sums(mesh_lanes, terms_mesh.at[layer - 1], lambda at: table[at], 4)
+            edge_sums(layer, mesh_lanes, terms_mesh, lambda at: table[at], 4)
 
         ends = 2 if layer == 0 else 6
+        sum_copies = []
+        for c in range(chunks):
+            for k in range(CHUNK * c, CHUNK * (c + 1)):
+                share_out[layer, k] = sums[plan[ends, (1 - sub) * half_tiles + k]]
+            part = pl.ds(CHUNK * c, CHUNK)
+            sum_copies.append(send(share_out.at[layer, part], share_in.at[layer, part], sibling))
         for k in range(half_tiles):
-            theirs = plan[ends, (1 - sub) * half_tiles + k]
-            share_out[layer, k] = sums[theirs]
-        sum_copy = send(share_out.at[layer], share_in.at[layer], sibling)
-        for k in range(half_tiles):
-            mine = plan[ends, sub * half_tiles + k]
             rows = slice(k * TILE, (k + 1) * TILE)
-            base[0, rows, :] = base[0, rows, :] + sums[mine]
+            base[0, rows, :] = base[0, rows, :] + sums[plan[ends, sub * half_tiles + k]]
+
+        hidden_copies = []
+        for c in range(chunks):
+            rows = pl.ds(chunk_rows * c, chunk_rows)
+            sum_copies[c].wait_recv()
+            hidden[layer, feat, rows, :] = silu(
+                base[0, rows, :]
+                + share_in[layer, CHUNK * c : CHUNK * (c + 1)].reshape(chunk_rows, width)
+                + node_bias[pl.ds(layer, 1), :]
+            ).astype(BF16)
+            part = hidden.at[layer, feat, rows, :]
+            hidden_copies.append([send(part, part, {"feat": peer}) for peer in feat_peers])
         if layer == 0:
             share_weights = []
             for at in range(LAYERS):
@@ -373,56 +397,34 @@
                     share_weights[at].append(send(part, part, sibling))
             for copy in gain_copies:
                 copy.wait_recv()
-        sum_copy.wait_recv()
-        active = silu(
-            base[0]
-            + share_in[layer].reshape(half_rows, width)
-            + node_bias[pl.ds(layer, 1), :]
-        ).astype(BF16)
-        for f in range(n_feat):
-            hidden[layer, 0, f] = active[f * part_rows : (f + 1) * part_rows]
-        hidden_copies = [
-            send(hidden.at[layer, 0, peer], hidden.at[layer, 1, feat], {"feat": peer})
-            for peer in feat_peers
-        ]
-        hidden[layer, 1, feat] = hidden[layer, 0, feat]
-        for copy in hidden_copies:
-            copy.wait_recv()
         for copy in share_weights[layer]:
             copy.wait_recv()
-        whole_hidden = jnp.concatenate([hidden[layer, 1, f] for f in range(n_feat)], axis=1)
-        updates = [
-            jnp.dot(whole_hidden, output_w[f, layer], preferred_element_type=F32)
-            for f in range(n_feat)
-        ]
-        row_mean = sum(jnp.sum(u, axis=1, keepdims=True) for u in updates) / model_width
-        row_squares = sum(jnp.sum(u * u, axis=1, keepdims=True) for u in updates) / model_width
-        scale = lax.rsqrt(row_squares - row_mean * row_mean + EPSILON)
-        def part_of(source):
-            return pl.ds(
-                pl.multiple_of(sub * half_rows + source * part_rows, part_rows), part_rows
+
+        share_latent = []
+        for c in range(chunks):
+            rows = pl.ds(chunk_rows * c, chunk_rows)
+            for copy in hidden_copies[c]:
+                copy.wait_recv()
+            whole_hidden = jnp.concatenate(
+                [hidden[layer, f, rows, :] for f in range(n_feat)], axis=1
             )
-
-        mine = part_of(feat)
-        for f in range(n_feat):
-            normed = (updates[f] - row_mean) * scale * gain[f, pl.ds(layer, 1), :]
-            latents[layer + 1, f, mine, :] = (
-                latents[layer, f, mine, :].astype(F32) + normed
-            ).astype(BF16)
-        columns = (lambda device: pl.ds(0, n_feat)) if layer < LAYERS - 1 else (lambda device: device)
-        latent_copies = [
-            send(
-                latents.at[layer + 1, columns(peer), mine, :],
-                latents.at[layer + 1, columns(peer), mine, :],
-                {"feat": peer},
+            updates = [
+                jnp.dot(whole_hidden, output_w[f, layer], preferred_element_type=F32)
+                for f in range(n_feat)
+            ]
+            row_mean = sum(jnp.sum(u, axis=1, keepdims=True) for u in updates) / model_width
+            row_squares = sum(jnp.sum(u * u, axis=1, keepdims=True) for u in updates) / model_width
+            scale = lax.rsqrt(row_squares - row_mean * row_mean + EPSILON)
+            mine = pl.ds(
+                pl.multiple_of(sub * half_rows + c * chunk_rows, chunk_rows), chunk_rows
             )
-            for peer in feat_peers
-        ]
-        part = latents.at[layer + 1, columns(feat), mine, :]
-        share_latent = [send(part, part, sibling)]
-        for source, copy in zip(feat_sources, latent_copies):
-            copy.wait_recv()
-            part = latents.at[layer + 1, columns(feat), part_of(source), :]
+            for f in range(n_feat):
+                normed = (updates[f] - row_mean) * scale * gain[f, pl.ds(layer, 1), :]
+                latents[layer + 1, f, mine, :] = (
+                    latents[layer, f, mine, :].astype(F32) + normed
+                ).astype(BF16)
+            columns = pl.ds(0, n_feat) if layer < LAYERS - 1 else feat
+            part = latents.at[layer + 1, columns, mine, :]
             share_latent.append(send(part, part, sibling))
         for copy in share_latent:
             copy.wait_recv()
@@ -461,9 +463,9 @@
     enc_edges = encoder_lanes.shape[0]
     mesh_edges = mesh_lanes.shape[0]
     half_rows = mesh_rows // 2
-    part_rows = half_rows // n_feat
-    copies = 2 * n_dom + 16 + (n_feat - 1) * (2 + 2 * LAYERS + 1 + 3 * LAYERS) + 2 * LAYERS
-    copies += 6 * (LAYERS - 1)
+    chunks = half_rows // (CHUNK * TILE)
+    copies = 2 * n_dom + (n_feat - 1) * (3 + 2 * LAYERS + LAYERS * chunks)
+    copies += 2 * LAYERS * chunks + 6 * (LAYERS - 1)
     smem = pl.BlockSpec(memory_space=pltpu.SMEM)
     plan = pl.pallas_call(
         functools.partial(plan_kernel, n_dom, tile_count),
@@ -472,7 +474,7 @@
         out_specs=smem,
         scratch_shapes=[pltpu.SMEM((tile_count,), jnp.int32)],
         compiler_params=pltpu.CompilerParams(vmem_limit_bytes=VMEM_GRANT),
-    )(encoder_tiles, mesh_tiles, halo_tiles)
+    )(encoder_tiles, mesh_tiles, halo_tiles.transpose(2, 0, 1))
     vmem = pl.BlockSpec(memory_space=pltpu.VMEM)
     far = pl.BlockSpec(memory_space=pltpu.HBM)
     return pl.pallas_call(
@@ -503,12 +505,13 @@
             pltpu.VMEM((LAYERS - 1, 3, CAP, TILE // 2, width), BF16),
             pltpu.VMEM((tile_count, TILE, width), F32),
             pltpu.VMEM((1, half_rows, width), F32),
-            pltpu.VMEM((enc_edges, width), F32),
-            pltpu.VMEM((LAYERS - 1, mesh_edges, width), F32),
+            pltpu.VMEM((SPLIT_ROWS, enc_edges), BF16),
+            pltpu.VMEM((SPLIT_ROWS, mesh_edges), BF16),
+            pltpu.VMEM((LAYERS, SPLIT_ROWS, width), BF16),
             pltpu.VMEM((max(enc_edges, mesh_edges) // TILE + 1, TILE, width), F32),
             pltpu.VMEM((LAYERS, tile_count // 2, TILE, width), F32),
             pltpu.VMEM((LAYERS, tile_count // 2, TILE, width), F32),
-            pltpu.VMEM((LAYERS, 2, n_feat, part_rows, width), BF16),
+            pltpu.VMEM((LAYERS, n_feat, half_rows, width), BF16),
             pltpu.SemaphoreType.DMA((14,)),
             pltpu.SemaphoreType.DMA((copies,)),
             pltpu.SemaphoreType.DMA((copies,)),

time: 88.6 us -> 68.4 us (0.77)
  Pallas kernels: 85.2 us -> 66.4 us
  local copies, waits for them, and re-layouts: 3.12 us -> 1.77 us
    pallas_call x1, Pallas kernels: 82.3 us -> 63.5 us  [local(): pl.pallas_call(functools.partial(kernel, (n_dom, n_feat)), out_shape=jax....]
    unnamed x2 -> x1, local copies, waits for them, and re-layouts: 3.12 us -> 1.77 us
where the time goes in v3:
time: 68.4 us; the launch traced here: 68.1 us
  Pallas kernels  66.4 us (97%)
  local copies, waits for them, and re-layouts  1.77 us (3%)
    pallas_call x1, Pallas kernels, local(): pl.pallas_call(functools.partial(kernel, (n_dom, n_feat)), out_shape=jax....  63.5 us
    pallas_call x1, Pallas kernels, local(): pl.pallas_call(functools.partial(plan_kernel, n_dom, tile_count), out_sha...  2.88 us
    unnamed x1, local copies, waits for them, and re-layouts  1.77 us

profile of v3, /device:TPU:0, one launch (start us, length us, event | category | flops | bytes accessed | tf_op | source)
XLA Modules:
  0.0 68.1 jit_solution(14039061711231645268)
XLA Ops:
  0.0 2.9 %shard_map.163.plan = s32[9,32]{1,0:T(8,128)} custom-call(s32[2,32]{1,0:T(2,128)} %encoder_tiles.1, s32[2,24]{1,0:T(2,128)} %mesh_tiles.1, s32[3,1,4]{2,1,0:T(1,128)} %bitcast.7), custom_call_target="tpu_custom_call" | custom-call | tf_op jit(solution)/shard_map/pallas_call | solution.py:470
  2.9 63.5 %shard_map.164 = bf16[768,256]{1,0:T(8,128)(2,1)} custom-call(s32[9,32]{1,0:T(8,128)} %shard_map.163.plan, s32[16,128]{1,0:T(8,128)} %bitcast.5, s32[12,128]{1,0:T(8,128)} %bitcast.6, f32[4,2048]{1,0:T(4,128)} %far_encoder_geometry.1, f32[4,1536]{1,0:T(4,128)} %far_mesh_geometry.1, f32[3,4,256]{2,1,0:T(4,128)} %far_edge_weight.1, f32[3,256]{1,0:T(4,128)} %far_edge_bias.1, ...), custom_call_target="tpu_custom_call" | custom-call | tf_op jit(solution)/shard_map/pallas_call | solution.py:480
  66.4 1.8 %copy.19 = bf16[768,256]{1,0:T(8,128)(2,1)} copy(bf16[768,256]{1,0:T(8,128)(2,1)} %shard_map.164) | data formatting | bytes 786432

commit v4 on v3

--- a/solution.py
+++ b/solution.py
@@ -30,59 +30,11 @@
     )
 
 
-def plan_kernel(n_dom, tile_count, encoder_tiles, mesh_tiles, halo_tiles, plan, last):
-    dom = lax.axis_index("dom")
-    previous = lax.rem(dom + n_dom - 1, n_dom)
-    following = lax.rem(dom + 1, n_dom)
-
-    def chain(tiles, row):
-        blocks = tiles.shape[1]
-
-        def clear(t, carry):
-            last[t] = blocks
-            return carry
-
-        def follow(block, carry):
-            target = tiles[1, block]
-            plan[row + 1, block] = last[target]
-            plan[row + 3, block] = target
-            last[target] = block
-            return carry
-
-        def keep(t, carry):
-            plan[row + 2, t] = last[t]
-            return carry
-
-        lax.fori_loop(0, tile_count, clear, 0)
-        lax.fori_loop(0, blocks, follow, 0)
-        lax.fori_loop(0, tile_count, keep, 0)
-
-    def grid_place(block, carry):
-        plan[0, block] = encoder_tiles[0, block]
-        return carry
-
-    def mesh_place(block, carry):
-        tile = mesh_tiles[0, block]
-        beyond = jnp.maximum(tile - tile_count, 0)
-        owner = lax.div(beyond, CAP)
-        slot = lax.rem(beyond, CAP)
-        way = jnp.where(owner == previous, 0, jnp.where(owner == following, 1, 2))
-        plan[4, block] = jnp.where(tile < tile_count, tile, tile_count + CAP * way + slot)
-        return carry
-
-    lax.fori_loop(0, encoder_tiles.shape[1], grid_place, 0)
-    lax.fori_loop(0, mesh_tiles.shape[1], mesh_place, 0)
-    chain(encoder_tiles, 0)
-    chain(mesh_tiles, 4)
-    for way, step in enumerate((1, n_dom - 1, n_dom // 2)):
-        peer = lax.rem(dom + step, n_dom)
-        for slot in range(CAP):
-            plan[8, CAP * way + slot] = jnp.maximum(halo_tiles[slot, 0, peer], 0)
-
-
 def kernel(
     sizes,
-    plan,
+    encoder_tiles,
+    mesh_tiles,
+    halo_tiles,
     far_encoder_lanes,
     far_mesh_lanes,
     far_encoder_geometry,
@@ -98,6 +50,7 @@
     output_weight,
     norm_gain,
     out,
+    plan,
     encoder_lanes,
     mesh_lanes,
     encoder_geometry,
@@ -243,6 +196,41 @@
         weight_copies.append([send(part, part, {"feat": peer}) for peer in feat_peers])
     gain_copies = [send(gain.at[feat], gain.at[feat], {"feat": peer}) for peer in feat_peers]
 
+    def chain(tiles, row, place):
+        blocks = tiles.shape[1]
+
+        def follow(block, last):
+            target = tiles[1, block]
+            earlier = last[0]
+            for t in range(1, tile_count):
+                earlier = jnp.where(target == t, last[t], earlier)
+            plan[row, block] = place(tiles[0, block])
+            plan[row + 1, block] = earlier
+            plan[row + 3, block] = target
+            return tuple(jnp.where(target == t, block, last[t]) for t in range(tile_count))
+
+        last = lax.fori_loop(0, blocks, follow, (jnp.int32(blocks),) * tile_count)
+        for t in range(tile_count):
+            plan[row + 2, t] = last[t]
+
+    ways = (1, n_dom - 1, n_dom // 2)
+
+    def mesh_place(tile):
+        place = tile
+        for way, step in enumerate(ways):
+            first = tile_count + CAP * lax.rem(dom + n_dom - step, n_dom)
+            slot = tile - first
+            listed = jnp.logical_and(slot >= 0, slot < CAP)
+            place = jnp.where(listed, tile_count + CAP * way + slot, place)
+        return place
+
+    chain(encoder_tiles, 0, lambda tile: tile)
+    chain(mesh_tiles, 4, mesh_place)
+    for way, step in enumerate(ways):
+        peer = lax.rem(dom + step, n_dom)
+        for slot in range(CAP):
+            plan[8, CAP * way + slot] = jnp.maximum(halo_tiles[slot, 0, peer], 0)
+
     def pieces(value):
         high = value.astype(BF16).astype(F32)
         middle = (value - high).astype(BF16).astype(F32)
@@ -341,7 +329,7 @@
             table = tables[layer - 1]
             half = pl.ds(pl.multiple_of(sub * half_tile, half_tile), half_tile)
             halo_copies = []
-            for way, step in enumerate((1, n_dom - 1, n_dom // 2)):
+            for way, step in enumerate(ways):
                 peer = lax.rem(dom + step, n_dom)
                 for slot in range(CAP):
                     listed = local_table[plan[8, CAP * way + slot]]
@@ -467,22 +455,15 @@
     copies = 2 * n_dom + (n_feat - 1) * (3 + 2 * LAYERS + LAYERS * chunks)
     copies += 2 * LAYERS * chunks + 6 * (LAYERS - 1)
     smem = pl.BlockSpec(memory_space=pltpu.SMEM)
-    plan = pl.pallas_call(
-        functools.partial(plan_kernel, n_dom, tile_count),
-        out_shape=jax.ShapeDtypeStruct((9, max(enc_edges, mesh_edges) // TILE), jnp.int32),
-        in_specs=[smem] * 3,
-        out_specs=smem,
-        scratch_shapes=[pltpu.SMEM((tile_count,), jnp.int32)],
-        compiler_params=pltpu.CompilerParams(vmem_limit_bytes=VMEM_GRANT),
-    )(encoder_tiles, mesh_tiles, halo_tiles.transpose(2, 0, 1))
     vmem = pl.BlockSpec(memory_space=pltpu.VMEM)
     far = pl.BlockSpec(memory_space=pltpu.HBM)
     return pl.pallas_call(
         functools.partial(kernel, (n_dom, n_feat)),
         out_shape=jax.ShapeDtypeStruct((mesh_rows, width), BF16),
-        in_specs=[smem] + [far] * 14,
+        in_specs=[smem] * 3 + [far] * 14,
         out_specs=vmem,
         scratch_shapes=[
+            pltpu.SMEM((9, max(enc_edges, mesh_edges) // TILE), jnp.int32),
             pltpu.VMEM((enc_edges // (2 * TILE), 2 * TILE), jnp.int32),
             pltpu.VMEM((mesh_edges // (2 * TILE), 2 * TILE), jnp.int32),
             pltpu.VMEM(encoder_geometry.shape, F32),
@@ -520,7 +501,9 @@
             collective_id=0, has_side_effects=True, vmem_limit_bytes=VMEM_GRANT
         ),
     )(
-        plan,
+        encoder_tiles,
+        mesh_tiles,
+        halo_tiles.transpose(2, 0, 1),
         encoder_lanes.reshape(-1, 2 * TILE),
         mesh_lanes.reshape(-1, 2 * TILE),
         encoder_geometry,

time: 68.4 us -> 65.3 us (0.955)
  Pallas kernels: 66.4 us -> 63.4 us
    pallas_call x1 -> x0, Pallas kernels: 2.88 us -> none  [local(): pl.pallas_call(functools.partial(plan_kernel, n_dom, tile_count), out_sha...]
where the time goes in v4:
time: 65.3 us; the launch traced here: 65.2 us
  Pallas kernels  63.4 us (97%)
  local copies, waits for them, and re-layouts  1.77 us (3%)
    pallas_call x1, Pallas kernels, local(): pl.pallas_call(functools.partial(kernel, (n_dom, n_feat)), out_shape=jax....  63.4 us
    unnamed x1, local copies, waits for them, and re-layouts  1.77 us

profile of v4, /device:TPU:0, one launch (start us, length us, event | category | flops | bytes accessed | tf_op | source)
XLA Modules:
  0.0 65.2 jit_solution(5545794115588600796)
XLA Ops:
  0.0 63.4 %shard_map.163 = bf16[768,256]{1,0:T(8,128)(2,1)} custom-call(s32[2,32]{1,0:T(2,128)} %encoder_tiles.1, s32[2,24]{1,0:T(2,128)} %mesh_tiles.1, s32[3,1,4]{2,1,0:T(1,128)} %bitcast.7, s32[16,128]{1,0:T(8,128)} %bitcast.5, s32[12,128]{1,0:T(8,128)} %bitcast.6, f32[4,2048]{1,0:T(4,128)} %far_encoder_geometry.1, f32[4,1536]{1,0:T(4,128)} %far_mesh_geometry.1, ...), custom_call_target="tpu_custom_call" | custom-call | tf_op jit(solution)/shard_map/pallas_call | solution.py:460
  63.4 1.8 %copy.19 = bf16[768,256]{1,0:T(8,128)(2,1)} copy(bf16[768,256]{1,0:T(8,128)(2,1)} %shard_map.163) | data formatting | bytes 786432
